TPU v7x, 128 devices: a whole 4x4x4 slice. The times are simulated.
128 devices in a mesh: tm: 16 (over z_hi, y, core), pitch: 4 (over x), span: 2 (over z_lo).
Axes of the slice: x: 4, y: 4, z: 4 (z_hi: 2, z_lo: 2; z = z_hi * 2 + z_lo), core: 2. Of those that a mesh axis runs over, the one named last changes fastest.
Arguments:
- adjoint: float32 [16, 5, 64, 16, 256], P('tm', None, 'pitch', 'span'), may hold values from -6 to 6
- source: float32 [16, 5, 64, 16, 256], P('tm', None, 'pitch', 'span'), may hold values from -6 to 6
- face_jacobian: float32 [16, 3, 5, 5, 64, 16, 256], P('tm', None, None, None, 'pitch', 'span'), may hold values from -2 to 2
- dissipation: float32 [16, 3, 64, 16, 256], P('tm', None, 'pitch', 'span'), may hold values from 0.5 to 1.5
- cell_jacobian: float32 [16, 5, 5, 64, 16, 256], P('tm', None, None, 'pitch', 'span'), may hold values from -2 to 2
- pseudo_step: float32 [16, 64, 16, 256], P('tm', 'pitch', 'span'), may hold values from 0.02 to 0.1
Outputs:
- adjoint_next: float32 [16, 5, 64, 16, 256], P('tm', None, 'pitch', 'span')
- pseudo_residual: float32 [16, 5, 64, 16, 256], P('tm', None, 'pitch', 'span')
All inputs are finite; a program needn't handle non-finite values.
Results may differ from a plain program's by a relative error of at most 0.0001.
Values sent between devices are 32-bit elements; how exact they have to be, the bound alone decides.
A program may use at most 128 MiB of HBM per device.

v0:
```python
import math

import jax
import jax.numpy as jnp
from jax import lax
from jax.sharding import PartitionSpec as P

frequency = 0.5
viscosity = 0.2
section_weights = (0.6, 0.6, 1.0)


def passed_along(array, axis, by):
    count = lax.axis_size(axis)
    return lax.ppermute(array, axis, [(i, (i + by) % count) for i in range(count)])


def passed_along_2(value, axis, steps):
    count = lax.axis_size(axis)
    leading, last = (max(0, -steps), min(count, count - steps))
    return lax.ppermute(value, axis, [(source, source + steps) for source in range(leading, last)])


def spectral_table(row_index, col_index, total):
    offset = (row_index[:, None] - col_index[None, :]) % total
    angle = math.pi * jnp.where(offset == 0, 1, offset).astype(jnp.float32) / total
    parity = (1 - 2 * (offset % 2)).astype(jnp.float32)
    sine = jnp.sin(angle)
    cosine = jnp.cos(angle)
    off_diag = parity * (frequency * 0.5 * cosine / sine + viscosity * 0.5 / (sine * sine))
    on_diag = viscosity * (total * total / 12.0 + 1.0 / 6.0)
    return jnp.where(offset == 0, jnp.float32(on_diag), off_diag)


def face_terms(jac_dir, dissip_dir, difference):
    turned = jnp.einsum("tbaprx,tbprx->taprx", jac_dir, difference, precision=lax.Precision.HIGHEST)
    spread = dissip_dir[:, None] * difference
    return (0.5 * (turned + spread), 0.5 * (turned - spread))


def spectral_term(field):
    local_count = field.shape[0]
    total = local_count * lax.axis_size("tm")
    own_columns = lax.axis_index("tm") * local_count + jnp.arange(local_count, dtype=jnp.int32)
    portion = lax.all_gather(field, "tm", axis=0, tiled=True)
    row_index = jnp.arange(portion.shape[0], dtype=jnp.int32)
    table = spectral_table(row_index, own_columns, total)
    return jnp.einsum("mn,mfprx->nfprx", table, portion, precision=lax.Precision.HIGHEST)


def residual_of(field, source, face_jacobian, dissipation, cell_jacobian):
    span_cells = field.shape[3]
    axial_cells = field.shape[4]
    upward = passed_along(field[:, :, :1], "pitch", -1)
    neighbor = jnp.concatenate([field[:, :, 1:], upward], axis=2)
    forward_part, backward_part = face_terms(
        face_jacobian[:, 0], dissipation[:, 0], field - neighbor
    )
    carried = passed_along(backward_part[:, :, -1:], "pitch", 1)
    summed = forward_part + jnp.concatenate([carried, backward_part[:, :, :-1]], axis=2)
    upward = passed_along_2(field[:, :, :, :1], "span", -1)
    neighbor = jnp.concatenate([field[:, :, :, 1:], upward], axis=3)
    span_index = lax.axis_index("span") * span_cells + jnp.arange(span_cells, dtype=jnp.int32)
    validity = (span_index < span_cells * lax.axis_size("span") - 1).astype(jnp.float32)
    difference = (field - neighbor) * validity[None, None, None, :, None]
    forward_part, backward_part = face_terms(face_jacobian[:, 1], dissipation[:, 1], difference)
    carried = passed_along_2(backward_part[:, :, :, -1:], "span", 1)
    summed = summed + forward_part + jnp.concatenate([carried, backward_part[:, :, :, :-1]], axis=3)
    neighbor = jnp.concatenate([field[..., 1:], jnp.zeros_like(field[..., :1])], axis=4)
    validity = (jnp.arange(axial_cells) < axial_cells - 1).astype(jnp.float32)
    forward_part, backward_part = face_terms(
        face_jacobian[:, 2], dissipation[:, 2], (field - neighbor) * validity
    )
    shifted = jnp.concatenate(
        [jnp.zeros_like(backward_part[..., :1]), backward_part[..., :-1]], axis=4
    )
    summed = summed + forward_part + shifted
    summed = summed + jnp.einsum(
        "tbaprx,tbprx->taprx", cell_jacobian, field, precision=lax.Precision.HIGHEST
    )
    summed = summed + spectral_term(field)
    return summed - source


def local(adjoint, source, face_jacobian, dissipation, cell_jacobian, pseudo_step):
    first = residual_of(adjoint, source, face_jacobian, dissipation, cell_jacobian)
    current = adjoint - section_weights[0] * pseudo_step[:, None] * first
    for factor in section_weights[1:]:
        update = residual_of(current, source, face_jacobian, dissipation, cell_jacobian)
        current = adjoint - factor * pseudo_step[:, None] * update
    return (current, first)


def solution(mesh):
    in_specs = (
        P("tm", None, "pitch", "span", None),
        P("tm", None, "pitch", "span", None),
        P("tm", None, None, None, "pitch", "span", None),
        P("tm", None, "pitch", "span", None),
        P("tm", None, None, "pitch", "span", None),
        P("tm", "pitch", "span", None),
    )
    out_specs = (P("tm", None, "pitch", "span", None), P("tm", None, "pitch", "span", None))
    return jax.shard_map(local, mesh=mesh, in_specs=in_specs, out_specs=out_specs, check_vma=False)
```

profile of v0, /device:TPU:1, one launch (start us, length us, event | category | flops | bytes accessed | tf_op | source)
XLA Modules:
  0.0 322.8 jit_solution(3539031288119577065)
XLA Ops:
  9.4 3.3 %collective-permute-start = (f32[1,5,1,8,256]{4,2,3,1,0:T(1,128)}, f32[1,5,1,8,256]{4,2,3,1,0:T(1,128)}, u32[]{:S(2)}, u32[]{:S(2)}) collective-permute-start(f32[1,5,1,8,256]{4,2,3,1,0:T(1,128)} %copy.11), channel_id=1, source_target_pairs={{0,6},{2,0},{4,2},{6,4},{1,7},{3,1},{5,3},{7,5},{8,14},{10,8},{12,... | collective-permute-start | bytes 122888 | tf_op jit(solution)/shard_map/ppermute | solution.py:15
  14.5 1.3 collective-permute-start.2
  17.8 3.3 %fusion.6 = f32[16,8,256,5]{2,1,0,3:T(8,128)} fusion(f32[1,5,5,16,8,256]{5,4,3,2,1,0:T(8,128)} %param.10, f32[16,8,256,5]{2,1,0,3:T(8,128)} %bitcast.235), kind=kLoop, calls=%fused_computation.9 | loop fusion | flops 1474560 | bytes 4587520
  22.9 1.4 fusion.28
  25.5 5.4 %fusion.9 = (f32[16,8,256,5]{2,1,0,3:T(8,128)S(1)}, f32[16,8,256,5]{2,1,0,3:T(8,128)S(1)}, f32[16,8,256,5]{2,1,0,3:T(8,128)S(1)}) fusion(f32[1,3,5,5,16,8,256]{6,5,4,3,2,1,0:T(8,128)} %param.8, f32[16,8,256,5]{2,1,0,3:T(8,128)S(1)} %copy.138, f32[16,8,256,5]{2,1,0,3:T(8,128)S(1)} %copy.136, f32[16,8,256,5]{2,1,0,3:T(8,128)S(1)} %copy.137), kind=kLoop, calls=%fused_computation.15 | loop fusion | flops 4423680 | bytes 13762560
  33.7 5.4 %collective-permute-start.3 = (f32[1,5,16,1,256]{4,2,3,1,0:T(8,128)}, f32[1,5,16,1,256]{4,2,3,1,0:T(8,128)}, u32[]{:S(2)}, u32[]{:S(2)}) collective-permute-start(f32[1,5,16,1,256]{4,2,3,1,0:T(8,128)} %slice.161), channel_id=1, source_target_pairs={{0,1},{2,3},{4,5},{6,7},{8,9},{10,11},{12,13},{14,15},{16,17},{18,... | collective-permute-start | bytes 245768 | tf_op jit(solution)/shard_map/ppermute | solution.py:21
  40.4 55.3 %all-gather.4.cloned.1.call-done = f32[16,5,16,8,256]{4,3,2,1,0:T(8,128)} async-done(((f32[1,5,16,8,256]{4,3,2,1,0:T(8,128)}), f32[16,5,16,8,256]{4,3,2,1,0:T(8,128)}) %all-gather.4.cloned.1.call-update) | async-done | bytes 10485776 | tf_op jit(solution)/shard_map/all_gather | solution.py:45
  95.7 15.5 %fusion.4 = f32[1,5,16,8,256]{4,0,3,2,1:T(1,128)S(1)} fusion(f32[16,5,16,8,256]{4,3,2,1,0:T(8,128)} %all-gather.4.cloned.1.call-done, s32[]{:T(128)S(6)} %axis_index.17), kind=kOutput, calls=%fused_computation.4 | convolution fusion | flops 31457872 | bytes 11141124 | tf_op jit(solution)/shard_map/mn,mfprx->nfprx/dot_general | solution.py:48
  111.4 4.0 %multiply_subtract_fusion = (f32[1,5,16,8,256]{4,2,3,1,0:T(8,128)S(1)}, f32[1,5,16,8,256]{4,2,3,1,0:T(8,128)}) fusion(f32[16,8,256]{2,0,1:T(8,128)S(1)} %copy-done.45, f32[1,5,16,8,256]{4,3,2,1,0:T(8,128)S(1)} %copy-done, f32[1,5,16,8,256]{4,3,2,1,0:T(8,128)S(1)} %copy-done.11, f32[1,5,16,8,256]{4,0,3,2,1:T(1,128)S(1)} %fusion.4, ...), kind=kLoop, calls=%fused_computation.102 | loop fusion | flops 3276800 | bytes 10221056 | tf_op jit(solution)/shard_map/sub | solution.py:87
  115.4 1.2 copy.23
  116.7 2.5 collective-permute-start.4
  119.2 1.7 collective-permute-start.6
  121.4 3.3 %fusion.7 = f32[16,8,256,5]{2,1,0,3:T(8,128)} fusion(f32[1,5,5,16,8,256]{5,4,3,2,1,0:T(8,128)} %param.10, f32[16,8,256,5]{2,1,0,3:T(8,128)S(1)} %copy.143), kind=kLoop, calls=%fused_computation.10 | loop fusion | flops 1474560 | bytes 4587520
  126.7 1.2 slice-done.2
  127.9 1.4 fusion.10
  131.8 4.6 %collective-permute-start.7 = (f32[1,5,16,1,256]{4,2,3,1,0:T(8,128)}, f32[1,5,16,1,256]{4,2,3,1,0:T(8,128)}, u32[]{:S(2)}, u32[]{:S(2)}) collective-permute-start(f32[1,5,16,1,256]{4,2,3,1,0:T(8,128)} %slice.172), channel_id=1, source_target_pairs={{0,1},{2,3},{4,5},{6,7},{8,9},{10,11},{12,13},{14,15},{16,17},{18,... | collective-permute-start | bytes 245768 | tf_op jit(solution)/shard_map/ppermute | solution.py:21
  137.6 58.8 %all-gather.6.cloned.1.call-done = f32[16,5,16,8,256]{4,3,2,1,0:T(8,128)} async-done(((f32[1,5,16,8,256]{4,3,2,1,0:T(8,128)}), f32[16,5,16,8,256]{4,3,2,1,0:T(8,128)}) %all-gather.6.cloned.1.call-update) | async-done | bytes 10485776 | tf_op jit(solution)/shard_map/all_gather | solution.py:45
  196.4 15.5 %fusion.2 = f32[1,5,16,8,256]{4,0,3,2,1:T(1,128)S(1)} fusion(f32[16,5,16,8,256]{4,3,2,1,0:T(8,128)} %all-gather.6.cloned.1.call-done, s32[]{:T(128)S(6)} %axis_index.17), kind=kOutput, calls=%fused_computation.2 | convolution fusion | flops 31457872 | bytes 11141124 | tf_op jit(solution)/shard_map/mn,mfprx->nfprx/dot_general | solution.py:48
  212.1 3.4 %fusion.37 = f32[1,5,16,8,256]{4,2,3,1,0:T(8,128)S(1)} fusion(f32[1,5,15,8,256]{4,2,3,1,0:T(8,128)} %bitcast.246, f32[1,5,1,8,256]{4,2,3,1,0:T(1,128)} %collective-permute-done.5, f32[1,5,16,7,256]{4,2,3,1,0:T(8,128)S(1)} %slice-done.7, f32[1,5,16,1,256]{4,2,3,1,0:T(8,128)} %collective-permute-done.7, f32[1,5,16,8,256]{4,0,3,2,1:T(1,128)S(1)} %fusion.2, ...), kind=kLoop, calls=%fused_computation.57 | loop fusion | flops 3276800 | bytes 9565696 | tf_op jit(solution)/shard_map/sub | solution.py:90
  215.4 1.2 copy.26
  216.7 1.8 copy.8
  218.4 2.3 copy.30
  220.8 2.5 collective-permute-start.8
  223.3 1.5 collective-permute-start.10
  225.1 3.4 %fusion.8 = f32[16,8,256,5]{2,1,0,3:T(8,128)} fusion(f32[1,5,5,16,8,256]{5,4,3,2,1,0:T(8,128)} %param.10, f32[16,8,256,5]{2,1,0,3:T(8,128)S(1)} %copy.147), kind=kLoop, calls=%fused_computation.11 | loop fusion | flops 1474560 | bytes 4587520
  228.9 2.1 collective-permute-done.10
  232.6 1.4 fusion.11
  236.6 2.4 collective-permute-start.11
  240.3 55.8 %all-gather.8.cloned.1.call-done = f32[16,5,16,8,256]{4,3,2,1,0:T(8,128)} async-done(((f32[1,5,16,8,256]{4,3,2,1,0:T(8,128)}), f32[16,5,16,8,256]{4,3,2,1,0:T(8,128)}) %all-gather.8.cloned.1.call-update) | async-done | bytes 10485776 | tf_op jit(solution)/shard_map/all_gather | solution.py:45
  296.1 15.5 %fusion = f32[1,5,16,8,256]{4,0,3,2,1:T(1,128)S(1)} fusion(f32[16,5,16,8,256]{4,3,2,1,0:T(8,128)} %all-gather.8.cloned.1.call-done, s32[]{:T(128)S(6)} %axis_index.17), kind=kOutput, calls=%fused_computation | convolution fusion | flops 31457872 | bytes 11141124 | tf_op jit(solution)/shard_map/mn,mfprx->nfprx/dot_general | solution.py:48
  311.7 3.2 fusion.47
  314.9 1.2 copy.29
  (194 shorter events, 25.0 us)
Async XLA Ops:
  7.2 88.5 %all-gather.4.cloned.1.call-start = ((), (), s32[]{:S(2)}) async-start(), calls=%async_computation | async-start | bytes 11141120 | tf_op jit(solution)/shard_map/all_gather | solution.py:45
  7.9 188.5 %all-gather.6.cloned.1.call-start = ((), (), s32[]{:S(2)}) async-start(), calls=%async_computation.1 | async-start | bytes 11141120 | tf_op jit(solution)/shard_map/all_gather | solution.py:45
  9.4 13.5 %collective-permute-start = (f32[1,5,1,8,256]{4,2,3,1,0:T(1,128)}, f32[1,5,1,8,256]{4,2,3,1,0:T(1,128)}, u32[]{:S(2)}, u32[]{:S(2)}) collective-permute-start(f32[1,5,1,8,256]{4,2,3,1,0:T(1,128)} %copy.11), channel_id=1, source_target_pairs={{0,6},{2,0},{4,2},{6,4},{1,7},{3,1},{5,3},{7,5},{8,14},{10,8},{12,... | collective-permute-start | bytes 122888 | tf_op jit(solution)/shard_map/ppermute | solution.py:15
  14.5 8.4 %collective-permute-start.2 = (f32[1,5,16,1,256]{4,2,3,1,0:T(8,128)}, f32[1,5,16,1,256]{4,2,3,1,0:T(8,128)}, u32[]{:S(2)}, u32[]{:S(2)}) collective-permute-start(f32[1,5,16,1,256]{4,2,3,1,0:T(8,128)} %copy.203), channel_id=1, source_target_pairs={{1,0},{3,2},{5,4},{7,6},{9,8},{11,10},{13,12},{15,14},{17,16},{19,... | collective-permute-start | bytes 245768 | tf_op jit(solution)/shard_map/ppermute | solution.py:21
  22.2 89.1 %copy-start.3 = (f32[16,8,256]{2,0,1:T(8,128)}, f32[16,8,256]{2,0,1:T(8,128)S(1)}, u32[]{:S(2)}) copy-start(f32[16,8,256]{2,0,1:T(8,128)S(1)} %copy.17) | copy-start | bytes 393220
  33.7 77.6 %collective-permute-start.1 = (f32[1,5,1,8,256]{4,2,3,1,0:T(1,128)}, f32[1,5,1,8,256]{4,2,3,1,0:T(1,128)}, u32[]{:S(2)}, u32[]{:S(2)}) collective-permute-start(f32[1,5,1,8,256]{4,2,3,1,0:T(1,128)} %slice.157), channel_id=1, source_target_pairs={{0,2},{2,4},{4,6},{6,0},{1,3},{3,5},{5,7},{7,1},{8,10},{10,12},{12... | collective-permute-start | bytes 122888 | tf_op jit(solution)/shard_map/ppermute | solution.py:15
  33.7 77.6 %collective-permute-start.3 = (f32[1,5,16,1,256]{4,2,3,1,0:T(8,128)}, f32[1,5,16,1,256]{4,2,3,1,0:T(8,128)}, u32[]{:S(2)}, u32[]{:S(2)}) collective-permute-start(f32[1,5,16,1,256]{4,2,3,1,0:T(8,128)} %slice.161), channel_id=1, source_target_pairs={{0,1},{2,3},{4,5},{6,7},{8,9},{10,11},{12,13},{14,15},{16,17},{18,... | collective-permute-start | bytes 245768 | tf_op jit(solution)/shard_map/ppermute | solution.py:21
  95.7 15.6 %copy-start.11 = (f32[1,5,16,8,256]{4,3,2,1,0:T(8,128)S(1)}, f32[1,5,16,8,256]{4,3,2,1,0:T(8,128)}, u32[]{:S(2)}) copy-start(f32[1,5,16,8,256]{4,3,2,1,0:T(8,128)} %param.7) | copy-start | bytes 1966084
  95.7 15.6 %copy-start.29 = (f32[1,5,16,8,256]{4,2,3,1,0:T(8,128)S(1)}, f32[1,5,16,8,256]{4,2,3,1,0:T(8,128)}, u32[]{:S(2)}) copy-start(f32[1,5,16,8,256]{4,2,3,1,0:T(8,128)} %copy-done.28) | copy-start | bytes 1966084
  95.7 15.6 %copy-start.33 = (f32[16,8,256,5]{2,1,0,3:T(8,128)S(1)}, f32[16,8,256,5]{2,1,0,3:T(8,128)}, u32[]{:S(2)}) copy-start(f32[16,8,256,5]{2,1,0,3:T(8,128)} %fusion.6) | copy-start | bytes 1966084
  95.7 15.6 %copy-start.34 = (f32[1,5,16,8,255]{4,2,3,1,0:T(8,128)S(1)}, f32[1,5,16,8,255]{4,2,3,1,0:T(8,128)}, u32[]{:S(2)}) copy-start(f32[1,5,16,8,255]{4,2,3,1,0:T(8,128)} %fusion.20) | copy-start | bytes 1958404
  95.7 15.6 %slice-start.6 = ((f32[1,5,16,8,256]{4,2,3,1,0:T(8,128)}), f32[1,5,16,7,256]{4,2,3,1,0:T(8,128)S(1)}, s32[]{:S(2)}) async-start(f32[1,5,16,8,256]{4,2,3,1,0:T(8,128)} %copy-done.35), calls=%async_computation.9 | async-start | bytes 1146880 | tf_op jit(solution)/shard_map/slice | solution.py:68
  95.7 15.6 %copy-start.45 = (f32[16,8,256]{2,0,1:T(8,128)S(1)}, f32[16,8,256]{2,0,1:T(8,128)}, u32[]{:S(2)}) copy-start(f32[16,8,256]{2,0,1:T(8,128)} %copy.9) | copy-start | bytes 393220
  116.6 179.4 %all-gather.8.cloned.1.call-start = ((), (), s32[]{:S(2)}) async-start(), calls=%async_computation.2 | async-start | bytes 11141120 | tf_op jit(solution)/shard_map/all_gather | solution.py:45
  116.7 8.3 %collective-permute-start.4 = (f32[1,5,1,8,256]{4,2,3,1,0:T(1,128)S(1)}, f32[1,5,1,8,256]{4,2,3,1,0:T(1,128)S(1)}, u32[]{:S(2)}, u32[]{:S(2)}) collective-permute-start(f32[1,5,1,8,256]{4,2,3,1,0:T(1,128)S(1)} %slice.167), channel_id=1, source_target_pairs={{0,6},{2,0},{4,2},{6,4},{1,7},{3,1},{5,3},{7,5},{8,14},{10,8},{12,... | collective-permute-start | bytes 122888 | tf_op jit(solution)/shard_map/ppermute | solution.py:15
  119.2 5.9 %collective-permute-start.6 = (f32[1,5,16,1,256]{4,2,3,1,0:T(8,128)S(1)}, f32[1,5,16,1,256]{4,2,3,1,0:T(8,128)S(1)}, u32[]{:S(2)}, u32[]{:S(2)}) collective-permute-start(f32[1,5,16,1,256]{4,2,3,1,0:T(8,128)S(1)} %slice.171), channel_id=1, source_target_pairs={{1,0},{3,2},{5,4},{7,6},{9,8},{11,10},{13,12},{15,14},{17,16},{19,... | collective-permute-start | bytes 245768 | tf_op jit(solution)/shard_map/ppermute | solution.py:21
  131.0 81.0 %copy-start.32 = (f32[1,5,16,8,256]{4,2,3,1,0:T(8,128)}, f32[1,5,16,8,256]{4,2,3,1,0:T(8,128)S(1)}, u32[]{:S(2)}) copy-start(f32[1,5,16,8,256]{4,2,3,1,0:T(8,128)S(1)} %fusion.56) | copy-start | bytes 1966084
  131.8 80.2 %collective-permute-start.5 = (f32[1,5,1,8,256]{4,2,3,1,0:T(1,128)}, f32[1,5,1,8,256]{4,2,3,1,0:T(1,128)}, u32[]{:S(2)}, u32[]{:S(2)}) collective-permute-start(f32[1,5,1,8,256]{4,2,3,1,0:T(1,128)} %slice.168), channel_id=1, source_target_pairs={{0,2},{2,4},{4,6},{6,0},{1,3},{3,5},{5,7},{7,1},{8,10},{10,12},{12... | collective-permute-start | bytes 122888 | tf_op jit(solution)/shard_map/ppermute | solution.py:15
  131.8 80.2 %collective-permute-start.7 = (f32[1,5,16,1,256]{4,2,3,1,0:T(8,128)}, f32[1,5,16,1,256]{4,2,3,1,0:T(8,128)}, u32[]{:S(2)}, u32[]{:S(2)}) collective-permute-start(f32[1,5,16,1,256]{4,2,3,1,0:T(8,128)} %slice.172), channel_id=1, source_target_pairs={{0,1},{2,3},{4,5},{6,7},{8,9},{10,11},{12,13},{14,15},{16,17},{18,... | collective-permute-start | bytes 245768 | tf_op jit(solution)/shard_map/ppermute | solution.py:21
  137.6 74.4 %copy-start.2 = (f32[1,5,16,8,256]{4,2,3,1,0:T(8,128)S(1)}, f32[1,5,16,8,256]{4,2,3,1,0:T(8,128)}, u32[]{:S(2)}) copy-start(f32[1,5,16,8,256]{4,2,3,1,0:T(8,128)} %copy-done.1) | copy-start | bytes 1966084
  137.6 74.4 %copy-start.12 = (f32[1,5,16,8,256]{4,3,2,1,0:T(8,128)S(1)}, f32[1,5,16,8,256]{4,3,2,1,0:T(8,128)}, u32[]{:S(2)}) copy-start(f32[1,5,16,8,256]{4,3,2,1,0:T(8,128)} %param.7) | copy-start | bytes 1966084
  196.4 15.6 %copy-start.27 = (f32[16,8,256,5]{2,1,0,3:T(8,128)S(1)}, f32[16,8,256,5]{2,1,0,3:T(8,128)}, u32[]{:S(2)}) copy-start(f32[16,8,256,5]{2,1,0,3:T(8,128)} %copy-done.26) | copy-start | bytes 1966084
  196.4 15.6 %slice-start.7 = ((f32[1,5,16,8,256]{4,2,3,1,0:T(8,128)}), f32[1,5,16,7,256]{4,2,3,1,0:T(8,128)S(1)}, s32[]{:S(2)}) async-start(f32[1,5,16,8,256]{4,2,3,1,0:T(8,128)} %copy-done.36), calls=%async_computation.10 | async-start | bytes 1146880 | tf_op jit(solution)/shard_map/slice | solution.py:68
  196.4 15.6 %copy-start.39 = (f32[16,8,256,5]{2,1,0,3:T(8,128)S(1)}, f32[16,8,256,5]{2,1,0,3:T(8,128)}, u32[]{:S(2)}) copy-start(f32[16,8,256,5]{2,1,0,3:T(8,128)} %fusion.7) | copy-start | bytes 1966084
  196.4 15.6 %copy-start.41 = (f32[1,5,16,8,255]{4,2,3,1,0:T(8,128)S(1)}, f32[1,5,16,8,255]{4,2,3,1,0:T(8,128)}, u32[]{:S(2)}) copy-start(f32[1,5,16,8,255]{4,2,3,1,0:T(8,128)} %fusion.19) | copy-start | bytes 1958404
  196.4 15.6 %copy-start.46 = (f32[16,8,256]{2,0,1:T(8,128)S(1)}, f32[16,8,256]{2,0,1:T(8,128)}, u32[]{:S(2)}) copy-start(f32[16,8,256]{2,0,1:T(8,128)} %copy.9) | copy-start | bytes 393220
  216.7 15.8 %slice-start.3 = ((s8[9830400]{0:T(1024)(128)(4,1)}), s8[4194304]{0:T(1024)(128)(4,1)S(1)}, s32[]{:S(2)}) async-start(s8[9830400]{0:T(1024)(128)(4,1)} %bitcast.233), calls=%async_computation.6 | async-start | bytes 8388608
  220.8 8.1 %collective-permute-start.8 = (f32[1,5,1,8,256]{4,2,3,1,0:T(1,128)S(1)}, f32[1,5,1,8,256]{4,2,3,1,0:T(1,128)S(1)}, u32[]{:S(2)}, u32[]{:S(2)}) collective-permute-start(f32[1,5,1,8,256]{4,2,3,1,0:T(1,128)S(1)} %slice.178), channel_id=1, source_target_pairs={{0,6},{2,0},{4,2},{6,4},{1,7},{3,1},{5,3},{7,5},{8,14},{10,8},{12,... | collective-permute-start | bytes 122888 | tf_op jit(solution)/shard_map/ppermute | solution.py:15
  223.3 7.7 %collective-permute-start.10 = (f32[1,5,16,1,256]{4,2,3,1,0:T(8,128)S(1)}, f32[1,5,16,1,256]{4,2,3,1,0:T(8,128)S(1)}, u32[]{:S(2)}, u32[]{:S(2)}) collective-permute-start(f32[1,5,16,1,256]{4,2,3,1,0:T(8,128)S(1)} %slice.182), channel_id=1, source_target_pairs={{1,0},{3,2},{5,4},{7,6},{9,8},{11,10},{13,12},{15,14},{17,16},{19,... | collective-permute-start | bytes 245768 | tf_op jit(solution)/shard_map/ppermute | solution.py:21
  236.6 75.0 %collective-permute-start.9 = (f32[1,5,1,8,256]{4,2,3,1,0:T(1,128)}, f32[1,5,1,8,256]{4,2,3,1,0:T(1,128)}, u32[]{:S(2)}, u32[]{:S(2)}) collective-permute-start(f32[1,5,1,8,256]{4,2,3,1,0:T(1,128)} %slice.179), channel_id=1, source_target_pairs={{0,2},{2,4},{4,6},{6,0},{1,3},{3,5},{5,7},{7,1},{8,10},{10,12},{12... | collective-permute-start | bytes 122888 | tf_op jit(solution)/shard_map/ppermute | solution.py:15
  236.6 75.0 %collective-permute-start.11 = (f32[1,5,16,1,256]{4,2,3,1,0:T(8,128)}, f32[1,5,16,1,256]{4,2,3,1,0:T(8,128)}, u32[]{:S(2)}, u32[]{:S(2)}) collective-permute-start(f32[1,5,16,1,256]{4,2,3,1,0:T(8,128)} %slice.183), channel_id=1, source_target_pairs={{0,1},{2,3},{4,5},{6,7},{8,9},{10,11},{12,13},{14,15},{16,17},{18,... | collective-permute-start | bytes 245768 | tf_op jit(solution)/shard_map/ppermute | solution.py:21
  240.3 71.3 %copy-start.13 = (f32[1,5,16,8,256]{4,3,2,1,0:T(8,128)S(1)}, f32[1,5,16,8,256]{4,3,2,1,0:T(8,128)}, u32[]{:S(2)}) copy-start(f32[1,5,16,8,256]{4,3,2,1,0:T(8,128)} %param.7) | copy-start | bytes 1966084
  (40 other events, 373.4 us)
Sparse Core Ops, SparseCore 0:
  10.4 85.2 all-gather.3
  116.8 79.5 all-gather.5
  216.8 79.1 all-gather.7
where the time goes:
time: 329 us; the launch traced here: 323 us
  waiting for transfers between devices  173 us (53%)
  matrix products  46.5 us (14%)
  other arithmetic  36.8 us (11%)
  local copies, waits for them, and re-layouts  26.4 us (8%)
  starting transfers between devices  25.3 us (8%)
  between operations  15.1 us (5%)
    all_gather x3, waiting for transfers between devices, spectral_term(): portion = lax.all_gather(field, 'tm', axis=0, tiled=True)  170 us
    dot_general x3, matrix products, spectral_term(): jnp.einsum('mn,mfprx->nfprx', table, portion, precision=lax.Precision.HIG...  46.5 us
    unnamed x8, other arithmetic  18.2 us
    ppermute x6, starting transfers between devices, passed_along_2(): lax.ppermute(value, axis, [(source, source + steps) for source in range(l...  16.9 us
    unnamed x125, local copies, waits for them, and re-layouts  10.7 us
    ppermute x6, starting transfers between devices, passed_along(): lax.ppermute(array, axis, [(i, (i + by) % count) for i in range(count)])  8.27 us
  transfers between devices with their start and end apart: 15, of which 4 were waited for; matrix products, arithmetic and copies ran while one was open for 29% of the time, Pallas kernels for 0%

commit v1 on v0

v1 whole, which is shorter than its diff:
```python
import functools
import math

import jax
import jax.numpy as jnp
import numpy as np
from jax import lax
from jax.experimental import pallas as pl
from jax.experimental.pallas import tpu as pltpu
from jax.sharding import PartitionSpec as P

MESH = pl.DeviceIdType.MESH
FREQUENCY = 0.5
VISCOSITY = 0.2
WEIGHTS = (0.6, 0.6, 1.0)
FIELDS, TIMES, LAYERS, ROWS, LANES, HALVES = 5, 16, 16, 8, 128, 2
GROUPS = LAYERS // ROWS


def spectral_table():
    k = (np.arange(TIMES)[:, None] - np.arange(TIMES)[None, :]) % TIMES
    angle = np.pi * np.where(k == 0, 1, k) / TIMES
    off = 0.5 * (-1.0) ** k * (FREQUENCY * np.cos(angle) / np.sin(angle) + VISCOSITY / np.sin(angle) ** 2)
    return np.where(k == 0, VISCOSITY * (TIMES * TIMES / 12.0 + 1.0 / 6.0), off)


def coupled(values):
    table = spectral_table()
    half = TIMES // 2
    even = 0.5 * (table[:half, :half] + table[half:, :half])
    odd = 0.5 * (table[:half, :half] - table[half:, :half])
    sums = [values[m] + values[m + half] for m in range(half)]
    diffs = [values[m] - values[m + half] for m in range(half)]
    low, high = [], []
    for n in range(half):
        e = sums[0] * np.float32(even[0, n])
        o = diffs[0] * np.float32(odd[0, n])
        for m in range(1, half):
            e = e + sums[m] * np.float32(even[m, n])
            o = o + diffs[m] * np.float32(odd[m, n])
        low.append(e + o)
        high.append(e - o)
    return low + high


def kernel(
    adj_hbm, src_hbm, fj_hbm, ds_hbm, cj_hbm, ps_hbm,
    next_ref, res_ref,
    adj, cur, acc, inb, osrc, outb, fj, cj, ds, ps, src,
    lps, lpb, hss, hsb, lss, lsb,
    load_sem, in_send, in_recv, out_send, out_recv, halo_send, halo_recv,
):
    tm, pitch, span = lax.axis_index("tm"), lax.axis_index("pitch"), lax.axis_index("span")
    pitches = lax.axis_size("pitch")
    other = 1 - span
    up, down = lax.rem(pitch + 1, pitches), lax.rem(pitch + pitches - 1, pitches)
    zh, y, core = tm // 8, lax.rem(tm // 2, 4), lax.rem(tm, 2)

    def target(k):
        q, j = k // 4, k % 4
        dz, dy, dc = (j // 2 + q // 2) % 2, (2 + 3 * j) % 4, q % 2
        return (lax.rem(zh + dz, 2) * 4 + lax.rem(y + dy, 4)) * 2 + lax.rem(core + dc, 2)

    targets = [target(k) for k in range(TIMES)]
    row = lax.broadcasted_iota(jnp.int32, (ROWS, LANES), 0)
    lane = lax.broadcasted_iota(jnp.int32, (ROWS, LANES), 1)

    def cols(h):
        return slice(h * LANES, (h + 1) * LANES)

    def wait_for(ref, sem):
        pltpu.make_async_copy(ref, ref, sem).wait()

    for h in range(HALVES):
        for f in range(FIELDS):
            pltpu.make_async_copy(
                adj_hbm.at[0, f, :, :, cols(h)], adj.at[h, pl.ds(0, LAYERS), f], load_sem.at[0]
            ).start()
    loads = [
        pltpu.make_async_copy(a.at[0], b, load_sem.at[1 + i])
        for i, (a, b) in enumerate(
            ((src_hbm, src), (cj_hbm, cj), (fj_hbm, fj), (ds_hbm, ds), (ps_hbm, ps))
        )
    ]
    for copy in loads:
        copy.start()
    zero = jnp.zeros((ROWS, LANES), jnp.float32)
    for h in range(HALVES):
        for f in range(FIELDS):
            for g in range(GROUPS):
                hsb[h, f, g] = zero
                lsb[h, f, g] = zero

    barrier = pltpu.get_barrier_semaphore()
    for w in targets:
        pl.semaphore_signal(barrier, inc=1, device_id=(w, pitch, other), device_id_type=MESH)
    for p in (down, up):
        pl.semaphore_signal(barrier, inc=1, device_id=(tm, p, span), device_id_type=MESH)
    pl.semaphore_wait(barrier, TIMES + 2)
    wait_for(adj.at[:, pl.ds(0, LAYERS)], load_sem.at[0])

    def send_in(field, h, w):
        pltpu.make_async_remote_copy(
            src_ref=field.at[h, w], dst_ref=inb.at[h, tm],
            send_sem=in_send.at[h], recv_sem=in_recv.at[h],
            device_id=(w, pitch, other), device_id_type=MESH,
        ).start()

    def send_out(h, w):
        pltpu.make_async_remote_copy(
            src_ref=osrc.at[h, w], dst_ref=outb.at[h, tm],
            send_sem=out_send.at[h], recv_sem=out_recv.at[h],
            device_id=(w, pitch, other), device_id_type=MESH,
        ).start()

    def halo(i, source, dest, device):
        return pltpu.make_async_remote_copy(
            src_ref=source, dst_ref=dest, send_sem=halo_send.at[i], recv_sem=halo_recv.at[i],
            device_id=device, device_id_type=MESH,
        )

    def pack_first_rows(field):
        def body(g, c):
            for h in range(HALVES):
                for f in range(FIELDS):
                    tile = field[h, g * ROWS, f]
                    for j in range(1, ROWS):
                        tile = jnp.where(row == j, pltpu.roll(field[h, g * ROWS + j, f], j, 0), tile)
                    hss[h, f, g] = tile
            return c
        lax.fori_loop(0, GROUPS, body, 0)

    def face(d, l, h, diff):
        turned = []
        for a in range(FIELDS):
            s = fj[d, 0, a, l, :, cols(h)] * diff[0]
            for b in range(1, FIELDS):
                s = s + fj[d, b, a, l, :, cols(h)] * diff[b]
            turned.append(s)
        spread = [ds[d, l, :, cols(h)] * x for x in diff]
        return [t + s for t, s in zip(turned, spread)], [t - s for t, s in zip(turned, spread)]

    def pitch_face(field, l, h):
        diff = [0.5 * (field[h, l, f] - field[h, l + 1, f]) for f in range(FIELDS)]
        return face(0, l, h, diff)

    def near_layer(field, l, below, with_pitch):
        lows = []
        v = [[field[h, l, f] for f in range(FIELDS)] for h in range(HALVES)]
        carried = None
        for h in range(HALVES):
            total = [below[h * FIELDS + f] - src[f, l, :, cols(h)] for f in range(FIELDS)]
            for a in range(FIELDS):
                for b in range(FIELDS):
                    total[a] = total[a] + cj[b, a, l, :, cols(h)] * v[h][b]
            if with_pitch:
                upper, lower = pitch_face(field, l, h)
                total = [t + u for t, u in zip(total, upper)]
                lows += lower
            diff = []
            for f in range(FIELDS):
                after = pltpu.roll(v[h][f], LANES - 1, 1)
                if h + 1 < HALVES:
                    after = jnp.where(lane == LANES - 1, pltpu.roll(v[h + 1][f], LANES - 1, 1), after)
                    diff.append(0.5 * (v[h][f] - after))
                else:
                    diff.append(jnp.where(lane == LANES - 1, 0.0, 0.5 * (v[h][f] - after)))
            upper, lower = face(2, l, h, diff)
            turned = [pltpu.roll(x, 1, 1) for x in lower]
            for f in range(FIELDS):
                first = 0.0 if carried is None else carried[f]
                total[f] = total[f] + upper[f] + jnp.where(lane == 0, first, turned[f])
                acc[h, l, f] = total[f]
            carried = turned
        return lows

    def near(field):
        def body(l, below):
            return tuple(near_layer(field, l, below, True))
        below = lax.fori_loop(0, LAYERS - 1, body, (zero,) * (HALVES * FIELDS))
        near_layer(field, LAYERS - 1, below, False)

    def far(field):
        for h in range(HALVES):
            upper, lower = pitch_face(field, LAYERS - 1, h)
            for f in range(FIELDS):
                acc[h, LAYERS - 1, f] += upper[f]
                lps[h, f] = lower[f]
        halo(1, lps, lpb, (tm, up, span)).start()

        def body(g, c):
            for h in range(HALVES):
                packed = [zero] * FIELDS
                above = [hsb[h, f, g] for f in range(FIELDS)]
                for j in range(ROWS):
                    l = g * ROWS + j
                    diff = []
                    for f in range(FIELDS):
                        v = field[h, l, f]
                        edge = pltpu.roll(above[f], ROWS - 1 - j, 0) if j < ROWS - 1 else above[f]
                        after = jnp.where(row == ROWS - 1, edge, pltpu.roll(v, ROWS - 1, 0))
                        missing = (row == ROWS - 1) & (span == 1)
                        diff.append(jnp.where(missing, 0.0, 0.5 * (v - after)))
                    upper, lower = face(1, l, h, diff)
                    for f in range(FIELDS):
                        turned = pltpu.roll(lower[f], 1, 0)
                        acc[h, l, f] += upper[f] + jnp.where(row == 0, 0.0, turned)
                        moved = pltpu.roll(turned, j, 0) if j else turned
                        packed[f] = jnp.where(row == j, moved, packed[f])
                for f in range(FIELDS):
                    lss[h, f, g] = packed[f]
            return c
        lax.fori_loop(0, GROUPS, body, 0)

    def finish_acc():
        for h in range(HALVES):
            for f in range(FIELDS):
                acc[h, 0, f] += lpb[h, f]

        def body(g, c):
            for h in range(HALVES):
                for f in range(FIELDS):
                    below = lsb[h, f, g]
                    for j in range(ROWS):
                        moved = pltpu.roll(below, ROWS - j, 0) if j else below
                        acc[h, g * ROWS + j, f] += jnp.where(row == 0, moved, 0.0)
            return c
        lax.fori_loop(0, GROUPS, body, 0)

    def couple(h):
        def body(f, c):
            out = coupled([inb[h, m, f] for m in range(TIMES)])
            for n in range(TIMES):
                osrc[h, n, f] = out[n]
            return c
        lax.fori_loop(0, FIELDS, body, 0)
        for w in targets:
            send_out(h, w)

    for step, weight in enumerate(WEIGHTS):
        first, last = step == 0, step == len(WEIGHTS) - 1
        field = adj if first else cur
        if first:
            for w in targets:
                send_in(field, 0, w)
        halo(0, field.at[:, 0], field.at[:, LAYERS], (tm, down, span)).start()
        pack_first_rows(field)

        @pl.when(span == 1)
        def _():
            halo(2, hss, hsb, (tm, pitch, other)).start()

        if first:
            for w in targets:
                send_in(field, 1, w)
            for copy in loads:
                copy.wait()
        near(field)

        wait_for(inb.at[0], in_recv.at[0])
        couple(0)

        wait_for(field.at[:, LAYERS], halo_recv.at[0])

        @pl.when(span == 0)
        def _():
            wait_for(hsb, halo_recv.at[2])

        far(field)

        @pl.when(span == 0)
        def _():
            halo(3, lss, lsb, (tm, pitch, other)).start()

        wait_for(inb.at[1], in_recv.at[1])
        couple(1)

        wait_for(lpb, halo_recv.at[1])

        @pl.when(span == 1)
        def _():
            wait_for(lsb, halo_recv.at[3])

        finish_acc()

        wait_for(field.at[:, 0], halo_send.at[0])
        wait_for(lps, halo_send.at[1])

        @pl.when(span == 1)
        def _():
            wait_for(hss, halo_send.at[2])

        @pl.when(span == 0)
        def _():
            wait_for(lss, halo_send.at[3])

        for h in range(HALVES):
            wait_for(field.at[h, pl.ds(0, LAYERS)], in_send.at[h])
            wait_for(outb.at[h], out_recv.at[h])
            for w in targets:
                pace = ps[w, :, cols(h)] * np.float32(weight)
                for f in range(FIELDS):
                    residual = acc[h, w, f] + outb[h, w, f]
                    if first:
                        res_ref[0, f, w, :, cols(h)] = residual
                    new = adj[h, w, f] - pace * residual
                    if last:
                        next_ref[0, f, w, :, cols(h)] = new
                    else:
                        cur[h, w, f] = new
                if not last:
                    send_in(cur, h, w)
            wait_for(osrc.at[h], out_send.at[h])


def local(adjoint, source, face_jacobian, dissipation, cell_jacobian, pseudo_step):
    f32 = jnp.float32
    tile = (ROWS, LANES)
    block = (HALVES, LAYERS, FIELDS) + tile
    tall = (HALVES, LAYERS + 1, FIELDS) + tile
    edge = (HALVES, FIELDS) + tile
    rows = (HALVES, FIELDS, GROUPS) + tile
    vmem = [
        tall, tall, block, block, block, block,
        face_jacobian.shape[1:], cell_jacobian.shape[1:], dissipation.shape[1:],
        pseudo_step.shape[1:], source.shape[1:],
        edge, edge, rows, rows, rows, rows,
    ]
    dma = pltpu.SemaphoreType.DMA
    out = jax.ShapeDtypeStruct(adjoint.shape, f32)
    return pl.pallas_call(
        kernel,
        out_shape=(out, out),
        in_specs=[pl.BlockSpec(memory_space=pl.ANY)] * 6,
        out_specs=(pl.BlockSpec(memory_space=pltpu.VMEM),) * 2,
        scratch_shapes=[pltpu.VMEM(s, f32) for s in vmem]
        + [dma((6,)), dma((2,)), dma((2,)), dma((2,)), dma((2,)), dma((4,)), dma((4,))],
        compiler_params=pltpu.CompilerParams(
            collective_id=0, has_side_effects=True, vmem_limit_bytes=48 * 2**20
        ),
        name="adjoint_update",
    )(adjoint, source, face_jacobian, dissipation, cell_jacobian, pseudo_step)


def solution(mesh):
    in_specs = (
        P("tm", None, "pitch", "span", None),
        P("tm", None, "pitch", "span", None),
        P("tm", None, None, None, "pitch", "span", None),
        P("tm", None, "pitch", "span", None),
        P("tm", None, None, "pitch", "span", None),
        P("tm", "pitch", "span", None),
    )
    out_specs = (P("tm", None, "pitch", "span", None), P("tm", None, "pitch", "span", None))
    return jax.shard_map(local, mesh=mesh, in_specs=in_specs, out_specs=out_specs, check_vma=False)
```

time: 329 us -> 75.7 us (0.23)
  the two profiles are of different devices: /device:TPU:1 before, /device:TPU:47 now
where the time goes in v1:
time: 75.7 us; the launch traced here: 75.5 us
  Pallas kernels  69.1 us (91%)
  local copies, waits for them, and re-layouts  5.74 us (8%)
    pallas_call x1, Pallas kernels, local(): pl.pallas_call(kernel, out_shape=(out, out), in_specs=[pl.BlockSpec(memor...  69.1 us
    unnamed x10, local copies, waits for them, and re-layouts  5.74 us

profile of v1, /device:TPU:47, one launch (start us, length us, event | category | flops | bytes accessed | tf_op | source)
XLA Modules:
  0.0 75.5 jit_solution(1678115600486780973)
XLA Ops:
  0.6 0.0 copy-start
  0.6 1.1 %copy-done = f32[1,5,16,8,256]{4,3,2,1,0:T(8,128)S(1)} copy-done((f32[1,5,16,8,256]{4,3,2,1,0:T(8,128)S(1)}, f32[1,5,16,8,256]{4,3,2,1,0:T(8,128)}, u32[]{:S(2)}) %copy-start) | copy-done | bytes 655384
  1.7 0.0 copy-start.1
  1.7 1.1 %copy-done.1 = f32[1,5,16,8,256]{4,3,2,1,0:T(8,128)S(1)} copy-done((f32[1,5,16,8,256]{4,3,2,1,0:T(8,128)S(1)}, f32[1,5,16,8,256]{4,3,2,1,0:T(8,128)}, u32[]{:S(2)}) %copy-start.1) | copy-done | bytes 655384
  2.8 0.0 copy-start.2
  2.8 1.0 %copy-done.2 = f32[1,3,16,8,256]{4,3,2,1,0:T(8,128)S(1)} copy-done((f32[1,3,16,8,256]{4,3,2,1,0:T(8,128)S(1)}, f32[1,3,16,8,256]{4,3,2,1,0:T(8,128)}, u32[]{:S(2)}) %copy-start.2) | copy-done | bytes 393240
  3.8 0.0 copy-start.3
  3.8 0.9 %copy-done.3 = f32[1,16,8,256]{3,2,1,0:T(8,128)S(1)} copy-done((f32[1,16,8,256]{3,2,1,0:T(8,128)S(1)}, f32[1,16,8,256]{3,2,1,0:T(8,128)}, u32[]{:S(2)}) %copy-start.3) | copy-done | bytes 131096
  4.7 69.1 %adjoint_update.1 = (f32[1,5,16,8,256]{4,3,2,1,0:T(8,128)S(1)}, f32[1,5,16,8,256]{4,3,2,1,0:T(8,128)S(1)}) custom-call(f32[1,5,16,8,256]{4,3,2,1,0:T(8,128)S(1)} %copy-done, f32[1,5,16,8,256]{4,3,2,1,0:T(8,128)S(1)} %copy-done.1, f32[1,3,5,5,16,8,256]{6,5,4,3,2,1,0:T(8,128)} %fj_hbm.1, f32[1,3,16,8,256]{4,3,2,1,0:T(8,128)S(1)} %copy-done.2, ...), custom_call_target="tpu_custom_call" | custom-call | tf_op jit(solution)/shard_map/adjoint_update/pallas_call | solution.py:331
  73.8 0.8 %copy.10 = f32[1,5,16,8,256]{4,3,2,1,0:T(8,128)} copy(f32[1,5,16,8,256]{4,3,2,1,0:T(8,128)S(1)} %get-tuple-element.4) | data formatting | bytes 1310720
  74.6 0.8 %copy.11 = f32[1,5,16,8,256]{4,3,2,1,0:T(8,128)} copy(f32[1,5,16,8,256]{4,3,2,1,0:T(8,128)S(1)} %get-tuple-element.5) | data formatting | bytes 1310720
Async XLA Ops:
  0.6 1.1 %copy-start = (f32[1,5,16,8,256]{4,3,2,1,0:T(8,128)S(1)}, f32[1,5,16,8,256]{4,3,2,1,0:T(8,128)}, u32[]{:S(2)}) copy-start(f32[1,5,16,8,256]{4,3,2,1,0:T(8,128)} %adj_hbm.1) | copy-start | bytes 1966084
  1.7 1.1 %copy-start.1 = (f32[1,5,16,8,256]{4,3,2,1,0:T(8,128)S(1)}, f32[1,5,16,8,256]{4,3,2,1,0:T(8,128)}, u32[]{:S(2)}) copy-start(f32[1,5,16,8,256]{4,3,2,1,0:T(8,128)} %src_hbm.1) | copy-start | bytes 1966084
  2.8 1.0 %copy-start.2 = (f32[1,3,16,8,256]{4,3,2,1,0:T(8,128)S(1)}, f32[1,3,16,8,256]{4,3,2,1,0:T(8,128)}, u32[]{:S(2)}) copy-start(f32[1,3,16,8,256]{4,3,2,1,0:T(8,128)} %ds_hbm.1) | copy-start | bytes 1179652
  3.8 0.9 %copy-start.3 = (f32[1,16,8,256]{3,2,1,0:T(8,128)S(1)}, f32[1,16,8,256]{3,2,1,0:T(8,128)}, u32[]{:S(2)}) copy-start(f32[1,16,8,256]{3,2,1,0:T(8,128)} %ps_hbm.1) | copy-start | bytes 393220

commit v2 on v1

--- a/solution.py
+++ b/solution.py
@@ -82,22 +82,32 @@
             ((src_hbm, src), (cj_hbm, cj), (fj_hbm, fj), (ds_hbm, ds), (ps_hbm, ps))
         )
     ]
-    for copy in loads:
-        copy.start()
     zero = jnp.zeros((ROWS, LANES), jnp.float32)
     for h in range(HALVES):
         for f in range(FIELDS):
             for g in range(GROUPS):
                 hsb[h, f, g] = zero
                 lsb[h, f, g] = zero
+
+    def pack_first_rows(field, h):
+        for f in range(FIELDS):
+            for g in range(GROUPS):
+                tile = field[h, g * ROWS, f]
+                for j in range(1, ROWS):
+                    tile = jnp.where(row == j, pltpu.roll(field[h, g * ROWS + j, f], j, 0), tile)
+                hss[h, f, g] = tile
 
     barrier = pltpu.get_barrier_semaphore()
     for w in targets:
         pl.semaphore_signal(barrier, inc=1, device_id=(w, pitch, other), device_id_type=MESH)
     for p in (down, up):
         pl.semaphore_signal(barrier, inc=1, device_id=(tm, p, span), device_id_type=MESH)
+    wait_for(adj.at[:, pl.ds(0, LAYERS)], load_sem.at[0])
+    for copy in loads:
+        copy.start()
+    for h in range(HALVES):
+        pack_first_rows(adj, h)
     pl.semaphore_wait(barrier, TIMES + 2)
-    wait_for(adj.at[:, pl.ds(0, LAYERS)], load_sem.at[0])
 
     def send_in(field, h, w):
         pltpu.make_async_remote_copy(
@@ -113,22 +123,31 @@
             device_id=(w, pitch, other), device_id_type=MESH,
         ).start()
 
-    def halo(i, source, dest, device):
+    def halo(i, h, source, dest, device):
         return pltpu.make_async_remote_copy(
-            src_ref=source, dst_ref=dest, send_sem=halo_send.at[i], recv_sem=halo_recv.at[i],
+            src_ref=source, dst_ref=dest, send_sem=halo_send.at[i, h], recv_sem=halo_recv.at[i, h],
             device_id=device, device_id_type=MESH,
         )
 
-    def pack_first_rows(field):
-        def body(g, c):
-            for h in range(HALVES):
-                for f in range(FIELDS):
-                    tile = field[h, g * ROWS, f]
-                    for j in range(1, ROWS):
-                        tile = jnp.where(row == j, pltpu.roll(field[h, g * ROWS + j, f], j, 0), tile)
-                    hss[h, f, g] = tile
-            return c
-        lax.fori_loop(0, GROUPS, body, 0)
+    def rows_out(i, h, source, dest):
+        halo(i, h, source.at[h], dest.at[h], (tm, pitch, other)).start()
+
+    def send_field(field, h):
+        @pl.when(span == 1)
+        def _():
+            rows_out(2, h, hss, hsb)
+
+        halo(0, h, field.at[h, 0], field.at[h, LAYERS], (tm, down, span)).start()
+        for w in targets:
+            send_in(field, h, w)
+
+    def sent_field(field, h):
+        @pl.when(span == 1)
+        def _():
+            wait_for(hss.at[h], halo_send.at[2, h])
+
+        wait_for(field.at[h, 0], halo_send.at[0, h])
+        wait_for(field.at[h, pl.ds(0, LAYERS)], in_send.at[h])
 
     def face(d, l, h, diff):
         turned = []
@@ -170,7 +189,7 @@
             for f in range(FIELDS):
                 first = 0.0 if carried is None else carried[f]
                 total[f] = total[f] + upper[f] + jnp.where(lane == 0, first, turned[f])
-                acc[h, l, f] = total[f]
+                acc[h, l, f] += total[f]
             carried = turned
         return lows
 
@@ -180,137 +199,118 @@
         below = lax.fori_loop(0, LAYERS - 1, body, (zero,) * (HALVES * FIELDS))
         near_layer(field, LAYERS - 1, below, False)
 
-    def far(field):
-        for h in range(HALVES):
-            upper, lower = pitch_face(field, LAYERS - 1, h)
+    def far(field, h):
+        wait_for(field.at[h, LAYERS], halo_recv.at[0, h])
+        last_upper, lower = pitch_face(field, LAYERS - 1, h)
+        for f in range(FIELDS):
+            lps[h, f] = lower[f]
+        halo(1, h, lps.at[h], lpb.at[h], (tm, up, span)).start()
+
+        @pl.when(span == 0)
+        def _():
+            wait_for(hsb.at[h], halo_recv.at[2, h])
+
+        def body(g, c):
+            packed = [zero] * FIELDS
+            above = [hsb[h, f, g] for f in range(FIELDS)]
+            for j in range(ROWS):
+                l = g * ROWS + j
+                diff = []
+                for f in range(FIELDS):
+                    v = field[h, l, f]
+                    edge = pltpu.roll(above[f], ROWS - 1 - j, 0) if j < ROWS - 1 else above[f]
+                    after = jnp.where(row == ROWS - 1, edge, pltpu.roll(v, ROWS - 1, 0))
+                    missing = (row == ROWS - 1) & (span == 1)
+                    diff.append(jnp.where(missing, 0.0, 0.5 * (v - after)))
+                upper, lower = face(1, l, h, diff)
+                for f in range(FIELDS):
+                    turned = pltpu.roll(lower[f], 1, 0)
+                    acc[h, l, f] = upper[f] + jnp.where(row == 0, 0.0, turned)
+                    moved = pltpu.roll(turned, j, 0) if j else turned
+                    packed[f] = jnp.where(row == j, moved, packed[f])
             for f in range(FIELDS):
-                acc[h, LAYERS - 1, f] += upper[f]
-                lps[h, f] = lower[f]
-        halo(1, lps, lpb, (tm, up, span)).start()
-
-        def body(g, c):
-            for h in range(HALVES):
-                packed = [zero] * FIELDS
-                above = [hsb[h, f, g] for f in range(FIELDS)]
-                for j in range(ROWS):
-                    l = g * ROWS + j
-                    diff = []
-                    for f in range(FIELDS):
-                        v = field[h, l, f]
-                        edge = pltpu.roll(above[f], ROWS - 1 - j, 0) if j < ROWS - 1 else above[f]
-                        after = jnp.where(row == ROWS - 1, edge, pltpu.roll(v, ROWS - 1, 0))
-                        missing = (row == ROWS - 1) & (span == 1)
-                        diff.append(jnp.where(missing, 0.0, 0.5 * (v - after)))
-                    upper, lower = face(1, l, h, diff)
-                    for f in range(FIELDS):
-                        turned = pltpu.roll(lower[f], 1, 0)
-                        acc[h, l, f] += upper[f] + jnp.where(row == 0, 0.0, turned)
-                        moved = pltpu.roll(turned, j, 0) if j else turned
-                        packed[f] = jnp.where(row == j, moved, packed[f])
-                for f in range(FIELDS):
-                    lss[h, f, g] = packed[f]
+                lss[h, f, g] = packed[f]
             return c
         lax.fori_loop(0, GROUPS, body, 0)
 
-    def finish_acc():
-        for h in range(HALVES):
-            for f in range(FIELDS):
-                acc[h, 0, f] += lpb[h, f]
-
-        def body(g, c):
-            for h in range(HALVES):
-                for f in range(FIELDS):
-                    below = lsb[h, f, g]
-                    for j in range(ROWS):
-                        moved = pltpu.roll(below, ROWS - j, 0) if j else below
-                        acc[h, g * ROWS + j, f] += jnp.where(row == 0, moved, 0.0)
-            return c
-        lax.fori_loop(0, GROUPS, body, 0)
-
-    def couple(h):
+        @pl.when(span == 0)
+        def _():
+            rows_out(3, h, lss, lsb)
+
+        for f in range(FIELDS):
+            acc[h, LAYERS - 1, f] += last_upper[f]
+
+    def couple(h, first):
         def body(f, c):
             out = coupled([inb[h, m, f] for m in range(TIMES)])
             for n in range(TIMES):
                 osrc[h, n, f] = out[n]
             return c
+        if not first:
+            wait_for(osrc.at[h], out_send.at[h])
         lax.fori_loop(0, FIELDS, body, 0)
         for w in targets:
             send_out(h, w)
 
+    def update(field, h, weight, first, last):
+        wait_for(lpb.at[h], halo_recv.at[1, h])
+
+        @pl.when(span == 1)
+        def _():
+            wait_for(lsb.at[h], halo_recv.at[3, h])
+
+        wait_for(outb.at[h], out_recv.at[h])
+        sent_field(field, h)
+        wait_for(lps.at[h], halo_send.at[1, h])
+
+        @pl.when(span == 0)
+        def _():
+            wait_for(lss.at[h], halo_send.at[3, h])
+
+        for g in range(GROUPS):
+            below = [lsb[h, f, g] for f in range(FIELDS)]
+            packed = [None] * FIELDS
+            for j in range(ROWS):
+                l = g * ROWS + j
+                pace = ps[l, :, cols(h)] * np.float32(weight)
+                for f in range(FIELDS):
+                    moved = pltpu.roll(below[f], ROWS - j, 0) if j else below[f]
+                    residual = acc[h, l, f] + outb[h, l, f] + jnp.where(row == 0, moved, 0.0)
+                    if l == 0:
+                        residual = residual + lpb[h, f]
+                    if first:
+                        res_ref[0, f, l, :, cols(h)] = residual
+                    new = adj[h, l, f] - pace * residual
+                    if last:
+                        next_ref[0, f, l, :, cols(h)] = new
+                    else:
+                        cur[h, l, f] = new
+                        packed[f] = jnp.where(row == j, pltpu.roll(new, j, 0), packed[f]) if j else new
+            if not last:
+                for f in range(FIELDS):
+                    hss[h, f, g] = packed[f]
+        if not last:
+            send_field(cur, h)
+
+    send_field(adj, 0)
+    for copy in loads:
+        copy.wait()
+    send_field(adj, 1)
+
     for step, weight in enumerate(WEIGHTS):
         first, last = step == 0, step == len(WEIGHTS) - 1
         field = adj if first else cur
-        if first:
-            for w in targets:
-                send_in(field, 0, w)
-        halo(0, field.at[:, 0], field.at[:, LAYERS], (tm, down, span)).start()
-        pack_first_rows(field)
-
-        @pl.when(span == 1)
-        def _():
-            halo(2, hss, hsb, (tm, pitch, other)).start()
-
-        if first:
-            for w in targets:
-                send_in(field, 1, w)
-            for copy in loads:
-                copy.wait()
+        wait_for(inb.at[0], in_recv.at[0])
+        couple(0, first)
+        for h in range(HALVES):
+            far(field, h)
         near(field)
-
-        wait_for(inb.at[0], in_recv.at[0])
-        couple(0)
-
-        wait_for(field.at[:, LAYERS], halo_recv.at[0])
-
-        @pl.when(span == 0)
-        def _():
-            wait_for(hsb, halo_recv.at[2])
-
-        far(field)
-
-        @pl.when(span == 0)
-        def _():
-            halo(3, lss, lsb, (tm, pitch, other)).start()
-
         wait_for(inb.at[1], in_recv.at[1])
-        couple(1)
-
-        wait_for(lpb, halo_recv.at[1])
-
-        @pl.when(span == 1)
-        def _():
-            wait_for(lsb, halo_recv.at[3])
-
-        finish_acc()
-
-        wait_for(field.at[:, 0], halo_send.at[0])
-        wait_for(lps, halo_send.at[1])
-
-        @pl.when(span == 1)
-        def _():
-            wait_for(hss, halo_send.at[2])
-
-        @pl.when(span == 0)
-        def _():
-            wait_for(lss, halo_send.at[3])
-
+        couple(1, first)
         for h in range(HALVES):
-            wait_for(field.at[h, pl.ds(0, LAYERS)], in_send.at[h])
-            wait_for(outb.at[h], out_recv.at[h])
-            for w in targets:
-                pace = ps[w, :, cols(h)] * np.float32(weight)
-                for f in range(FIELDS):
-                    residual = acc[h, w, f] + outb[h, w, f]
-                    if first:
-                        res_ref[0, f, w, :, cols(h)] = residual
-                    new = adj[h, w, f] - pace * residual
-                    if last:
-                        next_ref[0, f, w, :, cols(h)] = new
-                    else:
-                        cur[h, w, f] = new
-                if not last:
-                    send_in(cur, h, w)
-            wait_for(osrc.at[h], out_send.at[h])
+            update(field, h, weight, first, last)
+    for h in range(HALVES):
+        wait_for(osrc.at[h], out_send.at[h])
 
 
 def local(adjoint, source, face_jacobian, dissipation, cell_jacobian, pseudo_step):
@@ -334,12 +334,15 @@
         in_specs=[pl.BlockSpec(memory_space=pl.ANY)] * 6,
         out_specs=(pl.BlockSpec(memory_space=pltpu.VMEM),) * 2,
         scratch_shapes=[pltpu.VMEM(s, f32) for s in vmem]
-        + [dma((6,)), dma((2,)), dma((2,)), dma((2,)), dma((2,)), dma((4,)), dma((4,))],
+        + [dma((6,)), dma((2,)), dma((2,)), dma((2,)), dma((2,)), dma((4, 2)), dma((4, 2))],
         compiler_params=pltpu.CompilerParams(
             collective_id=0, has_side_effects=True, vmem_limit_bytes=48 * 2**20
         ),
         name="adjoint_update",
-    )(adjoint, source, face_jacobian, dissipation, cell_jacobian, pseudo_step)
+    )(*(
+        pltpu.with_memory_space_constraint(x, pltpu.HBM)
+        for x in (adjoint, source, face_jacobian, dissipation, cell_jacobian, pseudo_step)
+    ))
 
 
 def solution(mesh):

time: 75.7 us -> 61.7 us (0.82)
  the two profiles are of different devices: /device:TPU:47 before, /device:TPU:1 now
where the time goes in v2:
time: 61.7 us; the launch traced here: 61.5 us
  Pallas kernels  59.2 us (96%)
  local copies, waits for them, and re-layouts  1.67 us (3%)
  between operations  0.64 us (1%)
    pallas_call x1, Pallas kernels, local(): pl.pallas_call(kernel, out_shape=(out, out), in_specs=[pl.BlockSpec(memor...  59.2 us
    unnamed x2, local copies, waits for them, and re-layouts  1.67 us

profile of v2, /device:TPU:1, one launch (start us, length us, event | category | flops | bytes accessed | tf_op | source)
XLA Modules:
  0.0 61.5 jit_solution(10864883712502769268)
XLA Ops:
  0.6 59.2 %adjoint_update.1 = (f32[1,5,16,8,256]{4,3,2,1,0:T(8,128)S(1)}, f32[1,5,16,8,256]{4,3,2,1,0:T(8,128)S(1)}) custom-call(f32[1,5,16,8,256]{4,3,2,1,0:T(8,128)} %adj_hbm.1, f32[1,5,16,8,256]{4,3,2,1,0:T(8,128)} %src_hbm.1, f32[1,3,5,5,16,8,256]{6,5,4,3,2,1,0:T(8,128)} %fj_hbm.1, f32[1,3,16,8,256]{4,3,2,1,0:T(8,128)} %ds_hbm.1, ...), custom_call_target="tpu_custom_call" | custom-call | tf_op jit(solution)/shard_map/adjoint_update/pallas_call | solution.py:331
  59.9 0.8 %copy.10 = f32[1,5,16,8,256]{4,3,2,1,0:T(8,128)} copy(f32[1,5,16,8,256]{4,3,2,1,0:T(8,128)S(1)} %get-tuple-element.4) | data formatting | bytes 1310720
  60.7 0.8 %copy.11 = f32[1,5,16,8,256]{4,3,2,1,0:T(8,128)} copy(f32[1,5,16,8,256]{4,3,2,1,0:T(8,128)S(1)} %get-tuple-element.5) | data formatting | bytes 1310720

commit v3 on v2

--- a/solution.py
+++ b/solution.py
@@ -15,6 +15,9 @@
 WEIGHTS = (0.6, 0.6, 1.0)
 FIELDS, TIMES, LAYERS, ROWS, LANES, HALVES = 5, 16, 16, 8, 128, 2
 GROUPS = LAYERS // ROWS
+EARLY = 8
+FIRST = ("S0", "P1", "L", "Q1", "F0", "C0", "N", "F1", "C1", "U0", "U1")
+ORDER = ("F0", "C0", "N", "F1", "C1", "U0", "U1")
 
 
 def spectral_table():
@@ -107,6 +110,13 @@
         copy.start()
     for h in range(HALVES):
         pack_first_rows(adj, h)
+
+    def clear(l, c):
+        for h in range(HALVES):
+            for f in range(FIELDS):
+                acc[h, l, f] = zero
+        return c
+    lax.fori_loop(0, LAYERS, clear, 0)
     pl.semaphore_wait(barrier, TIMES + 2)
 
     def send_in(field, h, w):
@@ -132,13 +142,14 @@
     def rows_out(i, h, source, dest):
         halo(i, h, source.at[h], dest.at[h], (tm, pitch, other)).start()
 
-    def send_field(field, h):
-        @pl.when(span == 1)
-        def _():
-            rows_out(2, h, hss, hsb)
-
-        halo(0, h, field.at[h, 0], field.at[h, LAYERS], (tm, down, span)).start()
-        for w in targets:
+    def send_field(field, h, start=0, stop=TIMES):
+        if start == 0:
+            @pl.when(span == 1)
+            def _():
+                rows_out(2, h, hss, hsb)
+
+            halo(0, h, field.at[h, 0], field.at[h, LAYERS], (tm, down, span)).start()
+        for w in targets[start:stop]:
             send_in(field, h, w)
 
     def sent_field(field, h):
@@ -163,41 +174,41 @@
         diff = [0.5 * (field[h, l, f] - field[h, l + 1, f]) for f in range(FIELDS)]
         return face(0, l, h, diff)
 
-    def near_layer(field, l, below, with_pitch):
-        lows = []
-        v = [[field[h, l, f] for f in range(FIELDS)] for h in range(HALVES)]
-        carried = None
-        for h in range(HALVES):
-            total = [below[h * FIELDS + f] - src[f, l, :, cols(h)] for f in range(FIELDS)]
-            for a in range(FIELDS):
-                for b in range(FIELDS):
-                    total[a] = total[a] + cj[b, a, l, :, cols(h)] * v[h][b]
-            if with_pitch:
-                upper, lower = pitch_face(field, l, h)
-                total = [t + u for t, u in zip(total, upper)]
-                lows += lower
-            diff = []
-            for f in range(FIELDS):
-                after = pltpu.roll(v[h][f], LANES - 1, 1)
-                if h + 1 < HALVES:
-                    after = jnp.where(lane == LANES - 1, pltpu.roll(v[h + 1][f], LANES - 1, 1), after)
-                    diff.append(0.5 * (v[h][f] - after))
-                else:
-                    diff.append(jnp.where(lane == LANES - 1, 0.0, 0.5 * (v[h][f] - after)))
-            upper, lower = face(2, l, h, diff)
-            turned = [pltpu.roll(x, 1, 1) for x in lower]
-            for f in range(FIELDS):
-                first = 0.0 if carried is None else carried[f]
-                total[f] = total[f] + upper[f] + jnp.where(lane == 0, first, turned[f])
-                acc[h, l, f] += total[f]
-            carried = turned
-        return lows
-
     def near(field):
-        def body(l, below):
-            return tuple(near_layer(field, l, below, True))
-        below = lax.fori_loop(0, LAYERS - 1, body, (zero,) * (HALVES * FIELDS))
-        near_layer(field, LAYERS - 1, below, False)
+        def body(l, c, with_pitch):
+            carried = None
+            for h in range(HALVES):
+                v = [field[h, l, f] for f in range(FIELDS)]
+                diff = []
+                for f in range(FIELDS):
+                    after = pltpu.roll(v[f], LANES - 1, 1)
+                    if h + 1 < HALVES:
+                        beyond = pltpu.roll(field[h + 1, l, f], LANES - 1, 1)
+                        diff.append(0.5 * (v[f] - jnp.where(lane == LANES - 1, beyond, after)))
+                    else:
+                        diff.append(jnp.where(lane == LANES - 1, 0.0, 0.5 * (v[f] - after)))
+                upper, lower = face(2, l, h, diff)
+                turned = [pltpu.roll(x, 1, 1) for x in lower]
+                for f in range(FIELDS):
+                    first = 0.0 if carried is None else carried[f]
+                    total = acc[h, l, f] - src[f, l, :, cols(h)] + upper[f]
+                    for b in range(FIELDS):
+                        total = total + cj[b, f, l, :, cols(h)] * v[b]
+                    acc[h, l, f] = total + jnp.where(lane == 0, first, turned[f])
+                carried = turned
+                if with_pitch:
+                    upper, lower = pitch_face(field, l, h)
+                    for f in range(FIELDS):
+                        acc[h, l, f] += upper[f]
+                        acc[h, l + 1, f] += lower[f]
+            return c
+        def group(g, c):
+            for j in range(4):
+                body(g * 4 + j, 0, with_pitch=True)
+            return c
+        lax.fori_loop(0, LAYERS // 4 - 1, group, 0)
+        for l in range(LAYERS - 4, LAYERS):
+            body(l, 0, with_pitch=l < LAYERS - 1)
 
     def far(field, h):
         wait_for(field.at[h, LAYERS], halo_recv.at[0, h])
@@ -225,7 +236,7 @@
                 upper, lower = face(1, l, h, diff)
                 for f in range(FIELDS):
                     turned = pltpu.roll(lower[f], 1, 0)
-                    acc[h, l, f] = upper[f] + jnp.where(row == 0, 0.0, turned)
+                    acc[h, l, f] += upper[f] + jnp.where(row == 0, 0.0, turned)
                     moved = pltpu.roll(turned, j, 0) if j else turned
                     packed[f] = jnp.where(row == j, moved, packed[f])
             for f in range(FIELDS):
@@ -281,6 +292,7 @@
                     if first:
                         res_ref[0, f, l, :, cols(h)] = residual
                     new = adj[h, l, f] - pace * residual
+                    acc[h, l, f] = zero
                     if last:
                         next_ref[0, f, l, :, cols(h)] = new
                     else:
@@ -292,23 +304,30 @@
         if not last:
             send_field(cur, h)
 
-    send_field(adj, 0)
-    for copy in loads:
-        copy.wait()
-    send_field(adj, 1)
-
+    field = adj
     for step, weight in enumerate(WEIGHTS):
         first, last = step == 0, step == len(WEIGHTS) - 1
-        field = adj if first else cur
-        wait_for(inb.at[0], in_recv.at[0])
-        couple(0, first)
-        for h in range(HALVES):
-            far(field, h)
-        near(field)
-        wait_for(inb.at[1], in_recv.at[1])
-        couple(1, first)
-        for h in range(HALVES):
-            update(field, h, weight, first, last)
+        for what in FIRST if first else ORDER:
+            h = int(what[1:] or 0)
+            if what[0] == "S":
+                send_field(adj, h)
+            elif what[0] == "P":
+                send_field(adj, h, 0, EARLY)
+            elif what[0] == "Q":
+                send_field(adj, h, EARLY, TIMES)
+            elif what[0] == "L":
+                for copy in loads:
+                    copy.wait()
+            elif what[0] == "F":
+                far(field, h)
+            elif what[0] == "N":
+                near(field)
+            elif what[0] == "C":
+                wait_for(inb.at[h], in_recv.at[h])
+                couple(h, first)
+            else:
+                update(field, h, weight, first, last)
+        field = cur
     for h in range(HALVES):
         wait_for(osrc.at[h], out_send.at[h])
 

time: 61.7 us -> 60.9 us (0.987)
  Pallas kernels: 59.2 us -> 58.5 us
    pallas_call x1, Pallas kernels: 59.2 us -> 58.5 us  [local(): pl.pallas_call(kernel, out_shape=(out, out), in_specs=[pl.BlockSpec(memor...]
where the time goes in v3:
time: 60.9 us; the launch traced here: 60.8 us
  Pallas kernels  58.5 us (96%)
  local copies, waits for them, and re-layouts  1.67 us (3%)
  between operations  0.64 us (1%)
    pallas_call x1, Pallas kernels, local(): pl.pallas_call(kernel, out_shape=(out, out), in_specs=[pl.BlockSpec(memor...  58.5 us
    unnamed x2, local copies, waits for them, and re-layouts  1.67 us

profile of v3, /device:TPU:1, one launch (start us, length us, event | category | flops | bytes accessed | tf_op | source)
XLA Modules:
  0.0 60.8 jit_solution(8769575364628995418)
XLA Ops:
  0.6 58.5 %adjoint_update.1 = (f32[1,5,16,8,256]{4,3,2,1,0:T(8,128)S(1)}, f32[1,5,16,8,256]{4,3,2,1,0:T(8,128)S(1)}) custom-call(f32[1,5,16,8,256]{4,3,2,1,0:T(8,128)} %adj_hbm.1, f32[1,5,16,8,256]{4,3,2,1,0:T(8,128)} %src_hbm.1, f32[1,3,5,5,16,8,256]{6,5,4,3,2,1,0:T(8,128)} %fj_hbm.1, f32[1,3,16,8,256]{4,3,2,1,0:T(8,128)} %ds_hbm.1, ...), custom_call_target="tpu_custom_call" | custom-call | tf_op jit(solution)/shard_map/adjoint_update/pallas_call | solution.py:350
  59.1 0.8 %copy.10 = f32[1,5,16,8,256]{4,3,2,1,0:T(8,128)} copy(f32[1,5,16,8,256]{4,3,2,1,0:T(8,128)S(1)} %get-tuple-element.4) | data formatting | bytes 1310720
  59.9 0.8 %copy.11 = f32[1,5,16,8,256]{4,3,2,1,0:T(8,128)} copy(f32[1,5,16,8,256]{4,3,2,1,0:T(8,128)S(1)} %get-tuple-element.5) | data formatting | bytes 1310720

commit v4 on v3

--- a/solution.py
+++ b/solution.py
@@ -74,6 +74,19 @@
     def wait_for(ref, sem):
         pltpu.make_async_copy(ref, ref, sem).wait()
 
+    zero = jnp.zeros((ROWS, LANES), jnp.float32)
+    for h in range(HALVES):
+        for f in range(FIELDS):
+            for g in range(GROUPS):
+                hsb[h, f, g] = zero
+                lsb[h, f, g] = zero
+
+    barrier = pltpu.get_barrier_semaphore()
+    for w in targets:
+        pl.semaphore_signal(barrier, inc=1, device_id=(w, pitch, other), device_id_type=MESH)
+    for p in (down, up):
+        pl.semaphore_signal(barrier, inc=1, device_id=(tm, p, span), device_id_type=MESH)
+
     for h in range(HALVES):
         for f in range(FIELDS):
             pltpu.make_async_copy(
@@ -85,13 +98,6 @@
             ((src_hbm, src), (cj_hbm, cj), (fj_hbm, fj), (ds_hbm, ds), (ps_hbm, ps))
         )
     ]
-    zero = jnp.zeros((ROWS, LANES), jnp.float32)
-    for h in range(HALVES):
-        for f in range(FIELDS):
-            for g in range(GROUPS):
-                hsb[h, f, g] = zero
-                lsb[h, f, g] = zero
-
     def pack_first_rows(field, h):
         for f in range(FIELDS):
             for g in range(GROUPS):
@@ -100,11 +106,6 @@
                     tile = jnp.where(row == j, pltpu.roll(field[h, g * ROWS + j, f], j, 0), tile)
                 hss[h, f, g] = tile
 
-    barrier = pltpu.get_barrier_semaphore()
-    for w in targets:
-        pl.semaphore_signal(barrier, inc=1, device_id=(w, pitch, other), device_id_type=MESH)
-    for p in (down, up):
-        pl.semaphore_signal(barrier, inc=1, device_id=(tm, p, span), device_id_type=MESH)
     wait_for(adj.at[:, pl.ds(0, LAYERS)], load_sem.at[0])
     for copy in loads:
         copy.start()
@@ -292,10 +293,10 @@
                     if first:
                         res_ref[0, f, l, :, cols(h)] = residual
                     new = adj[h, l, f] - pace * residual
-                    acc[h, l, f] = zero
                     if last:
                         next_ref[0, f, l, :, cols(h)] = new
                     else:
+                        acc[h, l, f] = zero
                         cur[h, l, f] = new
                         packed[f] = jnp.where(row == j, pltpu.roll(new, j, 0), packed[f]) if j else new
             if not last:

time: 60.9 us -> 61.6 us (1.011)
    pallas_call x1, Pallas kernels: 58.5 us -> 59.1 us  [local(): pl.pallas_call(kernel, out_shape=(out, out), in_specs=[pl.BlockSpec(memor...]
where the time goes in v4:
time: 61.6 us; the launch traced here: 61.4 us
  Pallas kernels  59.1 us (96%)
  local copies, waits for them, and re-layouts  1.67 us (3%)
  between operations  0.64 us (1%)
    pallas_call x1, Pallas kernels, local(): pl.pallas_call(kernel, out_shape=(out, out), in_specs=[pl.BlockSpec(memor...  59.1 us
    unnamed x2, local copies, waits for them, and re-layouts  1.67 us

profile of v4, /device:TPU:1, one launch (start us, length us, event | category | flops | bytes accessed | tf_op | source)
XLA Modules:
  0.0 61.4 jit_solution(15797573003214210710)
XLA Ops:
  0.6 59.1 %adjoint_update.1 = (f32[1,5,16,8,256]{4,3,2,1,0:T(8,128)S(1)}, f32[1,5,16,8,256]{4,3,2,1,0:T(8,128)S(1)}) custom-call(f32[1,5,16,8,256]{4,3,2,1,0:T(8,128)} %adj_hbm.1, f32[1,5,16,8,256]{4,3,2,1,0:T(8,128)} %src_hbm.1, f32[1,3,5,5,16,8,256]{6,5,4,3,2,1,0:T(8,128)} %fj_hbm.1, f32[1,3,16,8,256]{4,3,2,1,0:T(8,128)} %ds_hbm.1, ...), custom_call_target="tpu_custom_call" | custom-call | tf_op jit(solution)/shard_map/adjoint_update/pallas_call | solution.py:351
  59.7 0.8 %copy.10 = f32[1,5,16,8,256]{4,3,2,1,0:T(8,128)} copy(f32[1,5,16,8,256]{4,3,2,1,0:T(8,128)S(1)} %get-tuple-element.4) | data formatting | bytes 1310720
  60.6 0.8 %copy.11 = f32[1,5,16,8,256]{4,3,2,1,0:T(8,128)} copy(f32[1,5,16,8,256]{4,3,2,1,0:T(8,128)S(1)} %get-tuple-element.5) | data formatting | bytes 1310720
